TPU v7x, 128 devices: a whole 4x4x4 slice. The times are simulated.
128 devices in a mesh: dp: 128 (over y, z, x, core).
Axes of the slice: x: 4, y: 4, z: 4, core: 2. Of those that a mesh axis runs over, the one named last changes fastest.
Arguments:
- clips: bfloat16 [131072, 1152], P('dp'), may hold values from -0.1875 to 0.1875
- captions: bfloat16 [131072, 1152], P('dp'), may hold values from -0.1875 to 0.1875
- positive: int32 [131072], P('dp'), may hold values from 0 to 131071, as said below
- log_scale: float32 [1], replicated, may hold values from 1.6 to 2.6
- bias: float32 [1], replicated, may hold values from -3 to -1
Outputs:
- clip_grad: bfloat16 [131072, 1152], P('dp')
- caption_grad: bfloat16 [131072, 1152], P('dp')
Inputs may be any that keep to these rules, and one draw needn't show every extreme that they name: For a clip row of block k, positive names a caption row of one of the blocks (k - s) mod (131072 / 1024) with 0 <= s < 4.
All inputs are finite; a program needn't handle non-finite values.
Results may differ from a plain program's by a relative error of at most 0.0048.
Values may be sent and summed in bfloat16 or wider, within the bound.
No kernel may reach another device: no remote copies, remote signals or barrier semaphores. Data moves between devices by JAX's collectives and lax.ppermute only.
A program may use at most 128 MiB of HBM per device.

v0:
```python
import jax
import jax.numpy as jnp
from jax import lax
from jax.sharding import PartitionSpec as P

STEPS = 4


def from_behind(value, axis, by):
    size = lax.axis_size(axis)
    return lax.ppermute(value, axis, [(i, (i + by) % size) for i in range(size)])


def shards(clips, captions, positive, log_scale, bias):
    rows = clips.shape[0]
    count = lax.axis_size("dp")
    mine = lax.axis_index("dp")
    scale = jnp.exp(log_scale[0])
    shift = bias[0]
    column = jnp.arange(rows, dtype=jnp.int32)
    clip_sum = jnp.zeros(clips.shape, jnp.float32)
    carried = jnp.zeros(clips.shape, jnp.float32)
    block = captions
    for offset in range(STEPS):
        if offset > 0:
            block = from_behind(block, "dp", 1)
        owner = (mine - offset) % count
        first = owner * rows
        logit = (
            scale
            * lax.dot_general(
                clips, block, (((1,), (1,)), ((), ())), preferred_element_type=jnp.float32
            )
            + shift
        )
        label = jnp.where(positive[:, None] == first + column[None, :], 1.0, -1.0).astype(
            jnp.float32
        )
        coef = (scale * (-label * jax.nn.sigmoid(-label * logit))).astype(jnp.bfloat16)
        clip_sum = clip_sum + jnp.dot(coef, block, preferred_element_type=jnp.float32)
        term = lax.dot_general(
            coef, clips, (((0,), (0,)), ((), ())), preferred_element_type=jnp.float32
        )
        if offset > 0:
            carried = from_behind(carried, "dp", 1)
        carried = carried + term
    home_sum = from_behind(carried.astype(jnp.bfloat16), "dp", 1 - STEPS).astype(carried.dtype)
    return (clip_sum.astype(jnp.bfloat16), home_sum.astype(jnp.bfloat16))


def solution(mesh):
    in_specs = (P("dp", None), P("dp", None), P("dp"), P(), P())
    out_specs = (P("dp", None), P("dp", None))
    return jax.shard_map(shards, mesh=mesh, in_specs=in_specs, out_specs=out_specs, check_vma=False)
```

profile of v0, /device:TPU:0, one launch (start us, length us, event | category | flops | bytes accessed | tf_op | source)
XLA Modules:
  0.0 361.5 jit_solution(3411606023836122582)
XLA Ops:
  0.6 0.0 copy-start
  2.2 0.2 copy-done
  2.3 6.0 %multiply_convert_fusion.3 = bf16[1024,1024]{1,0:T(8,128)(2,1)S(1)} fusion(bf16[1024,1152]{1,0:T(8,128)(2,1)S(1)} %copy-done, bf16[1024,1152]{1,0:T(8,128)(2,1)} %param.6, f32[]{:T(128)} %bitcast.26, s32[1024]{0:T(1024)S(1)} %iota_add_fusion.3, f32[]{:T(128)} %bitcast, s32[1024]{0:T(1024)} %param.7), kind=kOutput, calls=%fused_computation.6 | convolution fusion | flops 2428502016 | bytes 6823944 | tf_op jit(solution)/shard_map/dot_general | solution.py:31
  8.3 0.0 copy-start.4
  8.3 0.0 copy-start.1
  8.3 4.7 %fusion.3 = f32[1024,1152]{1,0:T(8,128)} fusion(bf16[1024,1024]{1,0:T(8,128)(2,1)S(1)} %multiply_convert_fusion.3, bf16[1024,1152]{1,0:T(8,128)(2,1)S(1)} %copy-done), kind=kOutput, calls=%fused_computation.14 | convolution fusion | flops 2415919104 | bytes 9175040 | tf_op jit(solution)/shard_map/dot_general | solution.py:41
  13.0 0.0 copy-done.4
  13.1 0.0 collective-permute-start.3
  13.1 1.7 collective-permute-start
  14.7 83.9 %collective-permute-done = bf16[1024,1152]{1,0:T(8,128)(2,1)} collective-permute-done((bf16[1024,1152]{1,0:T(8,128)(2,1)}, bf16[1024,1152]{1,0:T(8,128)(2,1)}, u32[]{:S(2)}, u32[]{:S(2)}) %collective-permute-start) | collective-permute-done | bytes 2359328 | tf_op jit(solution)/shard_map/ppermute | solution.py:11
  98.7 0.0 copy-done.1
  98.7 5.9 %multiply_convert_fusion.2 = bf16[1024,1024]{1,0:T(8,128)(2,1)S(1)} fusion(bf16[1024,1152]{1,0:T(8,128)(2,1)S(1)} %copy-done, bf16[1024,1152]{1,0:T(8,128)(2,1)} %collective-permute-done, s32[1024]{0:T(1024)S(1)} %iota_add_fusion.2, f32[]{:T(128)} %bitcast.29, f32[]{:T(128)} %bitcast, s32[1024]{0:T(1024)S(1)} %copy-done.1), kind=kOutput, calls=%fused_computation.5 | convolution fusion | flops 2428502016 | bytes 6823944 | tf_op jit(solution)/shard_map/dot_general | solution.py:31
  104.6 0.0 copy-start.2
  104.6 0.0 collective-permute-done.3
  104.6 7.1 %convolution_add_fusion = f32[1024,1152]{1,0:T(8,128)} fusion(f32[1024,1152]{1,0:T(8,128)} %collective-permute-done.3, bf16[1024,1024]{1,0:T(8,128)(2,1)S(1)} %multiply_convert_fusion.2, bf16[1024,1152]{1,0:T(8,128)(2,1)S(1)} %copy-done), kind=kOutput, calls=%fused_computation.2 | convolution fusion | flops 2417098752 | bytes 13893632 | tf_op jit(solution)/shard_map/dot_general | solution.py:41
  111.7 0.0 copy-done.2
  111.7 0.0 collective-permute-start.4
  111.7 0.0 collective-permute-start.1
  111.8 84.5 %collective-permute-done.1 = bf16[1024,1152]{1,0:T(8,128)(2,1)} collective-permute-done((bf16[1024,1152]{1,0:T(8,128)(2,1)}, bf16[1024,1152]{1,0:T(8,128)(2,1)}, u32[]{:S(2)}, u32[]{:S(2)}) %collective-permute-start.1) | collective-permute-done | bytes 2359328 | tf_op jit(solution)/shard_map/ppermute | solution.py:11
  196.3 5.9 %multiply_convert_fusion.1 = bf16[1024,1024]{1,0:T(8,128)(2,1)S(1)} fusion(bf16[1024,1152]{1,0:T(8,128)(2,1)S(1)} %copy-done, bf16[1024,1152]{1,0:T(8,128)(2,1)} %collective-permute-done.1, s32[1024]{0:T(1024)S(1)} %iota_add_fusion.1, f32[]{:T(128)} %bitcast.28, f32[]{:T(128)} %bitcast, s32[1024]{0:T(1024)S(1)} %copy-done.1), kind=kOutput, calls=%fused_computation.4 | convolution fusion | flops 2428502016 | bytes 6823944 | tf_op jit(solution)/shard_map/dot_general | solution.py:31
  202.2 0.0 copy-start.5
  202.3 3.0 fusion.4
  205.3 0.0 copy-done.5
  205.3 0.0 collective-permute-done.4
  205.3 5.4 %add.133 = f32[1024,1152]{1,0:T(8,128)} add(f32[1024,1152]{1,0:T(8,128)} %collective-permute-done.4, f32[1024,1152]{1,0:T(8,128)S(1)} %fusion.4) | non-fusion elementwise | flops 1179648 | bytes 14155776 | tf_op jit(solution)/shard_map/add | solution.py:46
  210.7 0.0 collective-permute-start.5
  210.7 0.0 collective-permute-start.2
  210.7 5.2 %fusion = f32[1024,1152]{1,0:T(8,128)S(1)} fusion(bf16[1024,1024]{1,0:T(8,128)(2,1)} %copy-done.4, bf16[1024,1152]{1,0:T(8,128)(2,1)} %param.6), kind=kOutput, calls=%fused_computation.11 | convolution fusion | flops 2415919104 | bytes 9175040 | tf_op jit(solution)/shard_map/dot_general | solution.py:40
  215.9 79.4 %collective-permute-done.2 = bf16[1024,1152]{1,0:T(8,128)(2,1)} collective-permute-done((bf16[1024,1152]{1,0:T(8,128)(2,1)}, bf16[1024,1152]{1,0:T(8,128)(2,1)}, u32[]{:S(2)}, u32[]{:S(2)}) %collective-permute-start.2) | collective-permute-done | bytes 2359328 | tf_op jit(solution)/shard_map/ppermute | solution.py:11
  295.2 5.9 %multiply_convert_fusion = bf16[1024,1024]{1,0:T(8,128)(2,1)S(1)} fusion(bf16[1024,1152]{1,0:T(8,128)(2,1)S(1)} %copy-done, bf16[1024,1152]{1,0:T(8,128)(2,1)} %collective-permute-done.2, s32[1024]{0:T(1024)S(1)} %iota_add_fusion, f32[]{:T(128)} %bitcast.27, f32[]{:T(128)} %bitcast, s32[1024]{0:T(1024)S(1)} %copy-done.1), kind=kOutput, calls=%fused_computation.3 | convolution fusion | flops 2428502016 | bytes 6823944 | tf_op jit(solution)/shard_map/dot_general | solution.py:31
  301.2 3.0 fusion.5
  304.2 0.0 copy-start.3
  304.2 0.0 collective-permute-done.5
  304.2 3.2 add_convert_fusion
  307.5 0.0 copy-start.6
  307.5 0.3 collective-permute-start.6
  307.8 0.0 copy-done.3
  307.8 4.7 %fusion.1 = f32[1024,1152]{1,0:T(8,128)S(1)} fusion(bf16[1024,1024]{1,0:T(8,128)(2,1)S(1)} %copy-done.3, bf16[1024,1152]{1,0:T(8,128)(2,1)} %collective-permute-done), kind=kOutput, calls=%fused_computation.12 | convolution fusion | flops 2415919104 | bytes 9175040 | tf_op jit(solution)/shard_map/dot_general | solution.py:40
  312.5 0.0 copy-done.6
  312.6 4.5 %fusion.2 = f32[1024,1152]{1,0:T(8,128)S(1)} fusion(bf16[1024,1024]{1,0:T(8,128)(2,1)S(1)} %copy-done.6, bf16[1024,1152]{1,0:T(8,128)(2,1)} %collective-permute-done.1), kind=kOutput, calls=%fused_computation.13 | convolution fusion | flops 2415919104 | bytes 9175040 | tf_op jit(solution)/shard_map/dot_general | solution.py:40
  317.1 5.9 %add_convert_fusion.1 = bf16[1024,1152]{1,0:T(8,128)(2,1)} fusion(f32[1024,1152]{1,0:T(8,128)S(1)} %fusion.2, f32[1024,1152]{1,0:T(8,128)S(1)} %fusion, f32[1024,1152]{1,0:T(8,128)S(1)} %fusion.1, bf16[1024,1024]{1,0:T(8,128)(2,1)S(1)} %multiply_convert_fusion, bf16[1024,1152]{1,0:T(8,128)(2,1)} %collective-permute-done.2), kind=kOutput, calls=%fused_computation.1 | convolution fusion | flops 2420637696 | bytes 20971520 | tf_op jit(solution)/shard_map/dot_general | solution.py:40
  323.1 37.0 %collective-permute-done.6 = bf16[1024,1152]{1,0:T(8,128)(2,1)S(1)} collective-permute-done((bf16[1024,1152]{1,0:T(8,128)(2,1)S(1)}, bf16[1024,1152]{1,0:T(8,128)(2,1)S(1)}, u32[]{:S(2)}, u32[]{:S(2)}) %collective-permute-start.6) | collective-permute-done | bytes 2359328 | tf_op jit(solution)/shard_map/ppermute | solution.py:11
  360.1 1.4 copy.10
  (4 shorter events, 0.0 us)
Async XLA Ops:
  0.6 1.7 copy-start
  8.3 4.7 %copy-start.4 = (bf16[1024,1024]{1,0:T(8,128)(2,1)}, bf16[1024,1024]{1,0:T(8,128)(2,1)S(1)}, u32[]{:S(2)}) copy-start(bf16[1024,1024]{1,0:T(8,128)(2,1)S(1)} %multiply_convert_fusion.3) | copy-start | bytes 6291460
  8.3 90.3 %copy-start.1 = (s32[1024]{0:T(1024)S(1)}, s32[1024]{0:T(1024)}, u32[]{:S(2)}) copy-start(s32[1024]{0:T(1024)} %param.7) | copy-start | bytes 12292
  13.1 91.6 %collective-permute-start.3 = (f32[1024,1152]{1,0:T(8,128)}, f32[1024,1152]{1,0:T(8,128)}, u32[]{:S(2)}, u32[]{:S(2)}) collective-permute-start(f32[1024,1152]{1,0:T(8,128)} %fusion.3), channel_id=1, source_target_pairs={{0,1},{1,2},{2,3},{3,4},{4,5},{5,6},{6,7},{7,8},{8,9},{9,10},{10,1... | collective-permute-start | bytes 14155784 | tf_op jit(solution)/shard_map/ppermute | solution.py:11
  13.1 85.6 %collective-permute-start = (bf16[1024,1152]{1,0:T(8,128)(2,1)}, bf16[1024,1152]{1,0:T(8,128)(2,1)}, u32[]{:S(2)}, u32[]{:S(2)}) collective-permute-start(bf16[1024,1152]{1,0:T(8,128)(2,1)} %param.6), channel_id=1, source_target_pairs={{0,1},{1,2},{2,3},{3,4},{4,5},{5,6},{6,7},{7,8},{8,9},{9,10},{10,1... | collective-permute-start | bytes 7077896 | tf_op jit(solution)/shard_map/ppermute | solution.py:11
  104.6 7.1 %copy-start.2 = (bf16[1024,1024]{1,0:T(8,128)(2,1)}, bf16[1024,1024]{1,0:T(8,128)(2,1)S(1)}, u32[]{:S(2)}) copy-start(bf16[1024,1024]{1,0:T(8,128)(2,1)S(1)} %multiply_convert_fusion.2) | copy-start | bytes 6291460
  111.7 93.5 %collective-permute-start.4 = (f32[1024,1152]{1,0:T(8,128)}, f32[1024,1152]{1,0:T(8,128)}, u32[]{:S(2)}, u32[]{:S(2)}) collective-permute-start(f32[1024,1152]{1,0:T(8,128)} %convolution_add_fusion), channel_id=1, source_target_pairs={{0,1},{1,2},{2,3},{3,4},{4,5},{5,6},{6,7},{7,8},{8,9},{9,10},{10,1... | collective-permute-start | bytes 14155784 | tf_op jit(solution)/shard_map/ppermute | solution.py:11
  111.7 84.6 %collective-permute-start.1 = (bf16[1024,1152]{1,0:T(8,128)(2,1)}, bf16[1024,1152]{1,0:T(8,128)(2,1)}, u32[]{:S(2)}, u32[]{:S(2)}) collective-permute-start(bf16[1024,1152]{1,0:T(8,128)(2,1)} %collective-permute-done), channel_id=1, source_target_pairs={{0,1},{1,2},{2,3},{3,4},{4,5},{5,6},{6,7},{7,8},{8,9},{9,10},{10,1... | collective-permute-start | bytes 7077896 | tf_op jit(solution)/shard_map/ppermute | solution.py:11
  202.2 3.0 copy-start.5
  210.7 93.5 %collective-permute-start.5 = (f32[1024,1152]{1,0:T(8,128)}, f32[1024,1152]{1,0:T(8,128)}, u32[]{:S(2)}, u32[]{:S(2)}) collective-permute-start(f32[1024,1152]{1,0:T(8,128)} %add.133), channel_id=1, source_target_pairs={{0,1},{1,2},{2,3},{3,4},{4,5},{5,6},{6,7},{7,8},{8,9},{9,10},{10,1... | collective-permute-start | bytes 14155784 | tf_op jit(solution)/shard_map/ppermute | solution.py:11
  210.7 84.6 %collective-permute-start.2 = (bf16[1024,1152]{1,0:T(8,128)(2,1)}, bf16[1024,1152]{1,0:T(8,128)(2,1)}, u32[]{:S(2)}, u32[]{:S(2)}) collective-permute-start(bf16[1024,1152]{1,0:T(8,128)(2,1)} %collective-permute-done.1), channel_id=1, source_target_pairs={{0,1},{1,2},{2,3},{3,4},{4,5},{5,6},{6,7},{7,8},{8,9},{9,10},{10,1... | collective-permute-start | bytes 7077896 | tf_op jit(solution)/shard_map/ppermute | solution.py:11
  304.2 3.6 copy-start.3
  307.5 5.1 %copy-start.6 = (bf16[1024,1024]{1,0:T(8,128)(2,1)S(1)}, bf16[1024,1024]{1,0:T(8,128)(2,1)}, u32[]{:S(2)}) copy-start(bf16[1024,1024]{1,0:T(8,128)(2,1)} %copy-done.5) | copy-start | bytes 6291460
  307.5 52.6 %collective-permute-start.6 = (bf16[1024,1152]{1,0:T(8,128)(2,1)S(1)}, bf16[1024,1152]{1,0:T(8,128)(2,1)S(1)}, u32[]{:S(2)}, u32[]{:S(2)}) collective-permute-start(bf16[1024,1152]{1,0:T(8,128)(2,1)S(1)} %add_convert_fusion), channel_id=1, source_target_pairs={{0,125},{1,126},{2,127},{3,0},{4,1},{5,2},{6,3},{7,4},{8,5},{9,6},... | collective-permute-start | bytes 7077896 | tf_op jit(solution)/shard_map/ppermute | solution.py:11
where the time goes:
time: 362 us; the launch traced here: 361 us
  waiting for transfers between devices  285 us (79%)
  matrix products  62 us (17%)
  other arithmetic  8.63 us (2%)
    ppermute x7, waiting for transfers between devices, from_behind(): lax.ppermute(value, axis, [(i, (i + by) % size) for i in range(size)])  285 us
    dot_general x4, matrix products, shards(): lax.dot_general(clips, block, (((1,), (1,)), ((), ())), preferred_element...  23.8 us
    dot_general x4, matrix products, shards(): jnp.dot(coef, block, preferred_element_type=jnp.float32)  20.4 us
    dot_general x4, matrix products, shards(): lax.dot_general(coef, clips, (((0,), (0,)), ((), ())), preferred_element_...  17.8 us
  transfers between devices with their start and end apart: 7, of which 4 were waited for; matrix products, arithmetic and copies ran while one was open for 12% of the time, Pallas kernels for 0%

commit v1 on v0

v1 whole, which is shorter than its diff:
```python
import functools

import jax
import jax.numpy as jnp
from jax import lax
from jax.experimental import pallas as pl
from jax.experimental.pallas import tpu as pltpu
from jax.sharding import PartitionSpec as P

TILE = 256
CHUNK = 256


def band_kernel(pairs, has_sum, scalars, rows, row_ids, *refs):
    cols = refs[: 2 * pairs]
    rest = refs[2 * pairs :]
    out = rest[-1]
    scale = scalars[0]
    shift = scalars[1]
    block = rows[...]
    ids = row_ids[...]
    total = rest[0][...] if has_sum else None
    work = []
    for p in range(pairs):
        height = cols[2 * p].shape[0]
        for j in range(height // CHUNK):
            work.append((cols[2 * p], cols[2 * p + 1], j * CHUNK))

    def logits(item):
        col, _, start = item
        return lax.dot_general(
            block,
            col[start : start + CHUNK, :],
            (((1,), (1,)), ((), ())),
            preferred_element_type=jnp.float32,
        )

    ahead = logits(work[0])
    for n, item in enumerate(work):
        now = ahead
        if n + 1 < len(work):
            ahead = logits(work[n + 1])
        col, col_ids, start = item
        hit = ids == col_ids[:, start : start + CHUNK]
        z = scale * now + shift
        share = 1.0 / (1.0 + jnp.exp(jnp.where(hit, z, -z)))
        coef = (jnp.where(hit, -scale, scale) * share).astype(jnp.bfloat16)
        term = jnp.dot(coef, col[start : start + CHUNK, :], preferred_element_type=jnp.float32)
        total = term if total is None else total + term
    out[...] = total.astype(out.dtype)


def band(scalars, rows, row_ids, cols, summed=None, dtype=jnp.float32):
    height, width = rows.shape
    pairs = len(cols)
    whole = lambda i: (0, 0)
    tile = lambda i: (i, 0)
    in_specs = [
        pl.BlockSpec(memory_space=pltpu.SMEM),
        pl.BlockSpec((TILE, width), tile),
        pl.BlockSpec((TILE, 1), tile),
    ]
    args = [scalars, rows, row_ids[:, None]]
    for col, col_ids in cols:
        in_specs += [pl.BlockSpec(col.shape, whole), pl.BlockSpec((1, col.shape[0]), whole)]
        args += [col, col_ids[None, :]]
    if summed is not None:
        in_specs.append(pl.BlockSpec((TILE, width), tile))
        args.append(summed)
    flops = 4 * pairs * height * height * width
    return pl.pallas_call(
        functools.partial(band_kernel, pairs, summed is not None),
        grid=(height // TILE,),
        out_shape=jax.ShapeDtypeStruct((height, width), dtype),
        in_specs=in_specs,
        out_specs=pl.BlockSpec((TILE, width), tile),
        compiler_params=pltpu.CompilerParams(vmem_limit_bytes=48 * 1024 * 1024),
        cost_estimate=pl.CostEstimate(
            flops=flops, bytes_accessed=8 * height * width, transcendentals=pairs * height * height
        ),
    )(*args)


def shards(clips, captions, positive, log_scale, bias):
    rows = clips.shape[0]
    count = lax.axis_size("dp")
    mine = lax.axis_index("dp")
    even = mine % 2 == 0
    scalars = jnp.concatenate([jnp.exp(log_scale), bias])
    evens = range(0, count, 2)
    odds = range(1, count, 2)

    def move(value, pairs):
        return lax.ppermute(value, "dp", [(i, j % count) for i, j in pairs])

    def swap(value):
        return move(value, [(i, i ^ 1) for i in range(count)])

    apart = [(i, i - 2) for i in evens] + [(i, i + 2) for i in odds]
    together = [(i, i + 2) for i in evens] + [(i, i - 2) for i in odds]

    def caption_ids(owner):
        return (owner % count) * rows + jnp.arange(rows, dtype=jnp.int32)

    next_clip = move(clips, [(i, i - 2) for i in evens])
    last_caption = move(captions, [(i, i + 2) for i in odds])

    next_pos = move(positive, [(i, i - 2) for i in range(count)])
    other_pos = swap(jnp.stack([positive, next_pos]))
    x_ids = jnp.where(even, caption_ids(mine), positive)
    y_ids = jnp.where(even, positive, caption_ids(mine))
    w_ids = jnp.where(even, other_pos[0], caption_ids(mine - 1))
    u1_ids = jnp.where(even, next_pos, caption_ids(mine - 2))
    v1_ids = jnp.where(even, caption_ids(mine - 1), other_pos[1])
    u2_ids = jnp.where(even, other_pos[1], caption_ids(mine - 3))
    v2_ids = jnp.where(even, caption_ids(mine - 2), next_pos)

    x = jnp.where(even, captions, clips)
    y = jnp.where(even, clips, captions)
    w = swap(x)
    gy = band(scalars, y, y_ids, [(x, x_ids)])
    gx = band(scalars, x, x_ids, [(y, y_ids), (w, w_ids)])

    v2 = move(x, together)

    u1 = jnp.where(even, next_clip, last_caption)
    v1 = swap(u1)
    gu = band(scalars, u1, u1_ids, [(v1, v1_ids)], dtype=jnp.bfloat16)
    back = move(gu, together)
    gx = band(scalars, x, x_ids, [(u1, u1_ids)], gx)
    gy = band(scalars, y, y_ids, [(v1, v1_ids)], gy)

    u2 = swap(v2)
    gy = band(scalars, y, y_ids, [(v2, v2_ids)], gy)
    gx = band(scalars, x, x_ids, [(u2, u2_ids)], gx, dtype=jnp.bfloat16)
    gy = (gy + back.astype(jnp.float32)).astype(jnp.bfloat16)
    return jnp.where(even, gy, gx), jnp.where(even, gx, gy)


def solution(mesh):
    in_specs = (P("dp", None), P("dp", None), P("dp"), P(), P())
    out_specs = (P("dp", None), P("dp", None))
    return jax.shard_map(shards, mesh=mesh, in_specs=in_specs, out_specs=out_specs, check_vma=False)
```

time: 362 us -> 159 us (0.44)
  waiting for transfers between devices: 285 us -> 40.2 us
  Pallas kernels: 0 us -> 76.8 us
  matrix products: 62 us -> 0 us
  starting transfers between devices: 2.04 us -> 21.9 us
  local copies, waits for them, and re-layouts: 1.61 us -> 5.59 us
    ppermute x7 -> x9, waiting for transfers between devices: 285 us -> 40.2 us  [move(): return lax.ppermute(value, 'dp', [(i, j % count) for i, j in pairs])]
    pallas_call x0 -> x7, Pallas kernels: none -> 76.8 us  [band(): pl.pallas_call(functools.partial(band_kernel, pairs, summed is not None),...]
    dot_general x12 -> x0, matrix products: 62 us -> none  [the longest x4 23.8 us: shards(): lax.dot_general(clips, block, (((1,), (1,)), ((), ())), preferred_element...]
    ppermute x7 -> x9, starting transfers between devices: 2.04 us -> 21.9 us  [move(): return lax.ppermute(value, 'dp', [(i, j % count) for i, j in pairs])]
    select_n x0 -> x6, other arithmetic: none -> 10.3 us  [the longest x1 4.98 us: shards(): y = jnp.where(even, clips, captions)]
    add x5 -> x0, other arithmetic: 5.4 us -> none  [the longest x1 5.38 us: shards(): carried = carried + term]
  transfers between devices with their start and end apart: 7 -> 9, of which waited for: 4 -> 2; matrix products, arithmetic and copies ran while one was open for 12% -> 5% of each run, Pallas kernels for 0% -> 49%
where the time goes in v1:
time: 159 us; the launch traced here: 157 us
  Pallas kernels  76.8 us (48%)
  waiting for transfers between devices  40.2 us (25%)
  starting transfers between devices  21.9 us (14%)
  other arithmetic  10.3 us (6%)
  local copies, waits for them, and re-layouts  5.59 us (4%)
  between operations  2.16 us (1%)
    pallas_call x7, Pallas kernels, band(): pl.pallas_call(functools.partial(band_kernel, pairs, summed is not None),...  76.8 us
    ppermute x9, waiting for transfers between devices, move(): return lax.ppermute(value, 'dp', [(i, j % count) for i, j in pairs])  40.2 us
    ppermute x9, starting transfers between devices, move(): return lax.ppermute(value, 'dp', [(i, j % count) for i, j in pairs])  21.9 us
    select_n x1, other arithmetic, shards(): y = jnp.where(even, clips, captions)  4.98 us
    unnamed x12, local copies, waits for them, and re-layouts  4.14 us
    select_n x1, other arithmetic, shards(): return (jnp.where(even, gy, gx), jnp.where(even, gx, gy))  3.32 us
  transfers between devices with their start and end apart: 9, of which 2 were waited for; matrix products, arithmetic and copies ran while one was open for 5% of the time, Pallas kernels for 49%

profile of v1, /device:TPU:0, one launch (start us, length us, event | category | flops | bytes accessed | tf_op | source)
XLA Modules:
  0.0 157.1 jit_solution(14842684621505327799)
XLA Ops:
  0.6 10.7 %collective-permute-start.2 = (bf16[1024,1152]{1,0:T(8,128)(2,1)}, bf16[1024,1152]{1,0:T(8,128)(2,1)S(1)}, u32[]{:S(2)}, u32[]{:S(2)}) collective-permute-start(bf16[1024,1152]{1,0:T(8,128)(2,1)} %param.5), channel_id=1, source_target_pairs={{0,126},{2,0},{4,2},{6,4},{8,6},{10,8},{12,10},{14,12},{16,14},{18... | collective-permute-start | bytes 7077896 | tf_op jit(solution)/shard_map/ppermute | solution.py:94
  11.3 2.1 %collective-permute-start.3 = (bf16[1024,1152]{1,0:T(8,128)(2,1)}, bf16[1024,1152]{1,0:T(8,128)(2,1)}, u32[]{:S(2)}, u32[]{:S(2)}) collective-permute-start(bf16[1024,1152]{1,0:T(8,128)(2,1)} %param.6), channel_id=1, source_target_pairs={{1,3},{3,5},{5,7},{7,9},{9,11},{11,13},{13,15},{15,17},{17,19},{19... | collective-permute-start | bytes 7077896 | tf_op jit(solution)/shard_map/ppermute | solution.py:94
  13.4 5.0 %broadcast_select_fusion.4 = (bf16[1024,1152]{1,0:T(8,128)(2,1)}, bf16[1024,1152]{1,0:T(8,128)(2,1)}) fusion(bf16[1024,1152]{1,0:T(8,128)(2,1)} %param.5, bf16[1024,1152]{1,0:T(8,128)(2,1)} %param.6, pred[]{:T(512)S(6)} %eq.12), kind=kLoop, calls=%fused_computation.5 | loop fusion | flops 2359296 | bytes 9437185 | tf_op jit(solution)/shard_map/jit(_where)/select_n | solution.py:119
  18.4 0.0 copy-start.5
  18.4 0.0 collective-permute-start
  18.4 40.1 %collective-permute-done.2 = bf16[1024,1152]{1,0:T(8,128)(2,1)S(1)} collective-permute-done((bf16[1024,1152]{1,0:T(8,128)(2,1)}, bf16[1024,1152]{1,0:T(8,128)(2,1)S(1)}, u32[]{:S(2)}, u32[]{:S(2)}) %collective-permute-start.2) | collective-permute-done | bytes 2359328 | tf_op jit(solution)/shard_map/ppermute | solution.py:94
  58.5 0.0 copy-start.4
  58.5 1.4 copy-done.4
  59.9 0.0 collective-permute-done.3
  59.9 1.9 %broadcast_select_fusion.2.rows.refs_0_ = bf16[1024,1152]{1,0:T(8,128)(2,1)S(1)} fusion(bf16[1024,1152]{1,0:T(8,128)(2,1)} %copy-done.4, bf16[1024,1152]{1,0:T(8,128)(2,1)} %collective-permute-done.3, pred[]{:T(512)S(6)} %eq.12), kind=kLoop, calls=%fused_computation.3 | loop fusion | flops 1179648 | bytes 7077889 | tf_op jit(solution)/shard_map/jit(_where)/select_n | solution.py:126
  61.8 0.1 collective-permute-start.4
  61.9 0.5 collective-permute-start.8
  62.4 0.0 copy-done.5
  62.4 7.8 %collective-permute-start.1 = (s32[1024]{0:T(1024)S(1)}, s32[1024]{0:T(1024)S(1)}, u32[]{:S(2)}, u32[]{:S(2)}) collective-permute-start(s32[1024]{0:T(1024)S(1)} %copy-done.5), channel_id=1, source_target_pairs={{0,126},{1,127},{2,0},{3,1},{4,2},{5,3},{6,4},{7,5},{8,6},{9,7},{1... | collective-permute-start | bytes 12296 | tf_op jit(solution)/shard_map/ppermute | solution.py:94
  71.6 0.2 copy.9.row_ids
  71.8 0.1 pad_maximum_fusion.scalars
  71.9 0.0 copy-start
  71.9 1.7 %copy-done = bf16[1024,1152]{1,0:T(8,128)(2,1)S(1)} copy-done((bf16[1024,1152]{1,0:T(8,128)(2,1)S(1)}, bf16[1024,1152]{1,0:T(8,128)(2,1)}, u32[]{:S(2)}) %copy-start) | copy-done | bytes 2359320
  73.5 10.6 %shard_map.68.refs_2_ = f32[1024,1152]{1,0:T(8,128)} custom-call(f32[2]{0:T(128)S(1)} %pad_maximum_fusion.scalars, bf16[1024,1152]{1,0:T(8,128)(2,1)S(1)} %copy-done, s32[1024,1]{1,0:T(8,128)S(1)} %copy.9.row_ids, bf16[1024,1152]{1,0:T(8,128)(2,1)} %get-tuple-element.5.refs_0_.rows, s32[1,1024]{1,0:T(1,128)S(1)} %bitcast.11), custom_call_target="tpu_custom_call" | custom-call | flops 4831838208 | bytes 9437184 | tf_op jit(solution)/shard_map/pallas_call | solution.py:71
  84.1 0.2 copy.13.row_ids
  84.4 0.0 collective-permute-done.1
  84.4 0.1 collective-permute-start.5
  84.5 1.0 copy.10.row_ids
  85.5 0.1 collective-permute-done.5
  85.7 0.0 collective-permute-done.refs_0_
  85.7 0.4 collective-permute-start.7
  86.1 0.0 collective-permute-done.4.refs_0_
  86.1 0.0 copy-start.2
  86.1 1.0 copy-done.2
  87.2 0.0 copy-start.1
  87.2 9.6 %shard_map.71 = bf16[1024,1152]{1,0:T(8,128)(2,1)S(1)} custom-call(f32[2]{0:T(128)S(1)} %pad_maximum_fusion.scalars, bf16[1024,1152]{1,0:T(8,128)(2,1)S(1)} %broadcast_select_fusion.2.rows.refs_0_, s32[1024,1]{1,0:T(8,128)S(1)} %copy-done.2, bf16[1024,1152]{1,0:T(8,128)(2,1)} %collective-permute-done.4.refs_0_, s32[1,1024]{1,0:T(1,128)S(1)} %get-tuple-element.6.refs_1_), custom_call_target="tpu_custom_call" | custom-call | flops 4831838208 | bytes 9437184 | tf_op jit(solution)/shard_map/pallas_call | solution.py:71
  96.8 0.3 collective-permute-start.6
  97.0 0.0 collective-permute-done.8.refs_2_
  97.1 0.0 copy-done.1
  97.1 16.8 %shard_map.72.refs_2_ = f32[1024,1152]{1,0:T(8,128)} custom-call(f32[2]{0:T(128)S(1)} %pad_maximum_fusion.scalars, bf16[1024,1152]{1,0:T(8,128)(2,1)} %get-tuple-element.5.refs_0_.rows, s32[1024,1]{1,0:T(8,128)S(1)} %copy.13.row_ids, bf16[1024,1152]{1,0:T(8,128)(2,1)S(1)} %copy-done.1, s32[1,1024]{1,0:T(1,128)S(1)} %bitcast.10, ...), custom_call_target="tpu_custom_call" | custom-call | flops 9663676416 | bytes 9437184 | tf_op jit(solution)/shard_map/pallas_call | solution.py:71
  113.9 9.8 %shard_map.73.refs_2_ = f32[1024,1152]{1,0:T(8,128)} custom-call(f32[2]{0:T(128)S(1)} %pad_maximum_fusion.scalars, bf16[1024,1152]{1,0:T(8,128)(2,1)} %get-tuple-element.5.refs_0_.rows, s32[1024,1]{1,0:T(8,128)S(1)} %copy.13.row_ids, bf16[1024,1152]{1,0:T(8,128)(2,1)S(1)} %broadcast_select_fusion.2.rows.refs_0_, s32[1,1024]{1,0:T(1,128)S(1)} %bitcast.14, ...), custom_call_target="tpu_custom_call" | custom-call | flops 4831838208 | bytes 9437184 | tf_op jit(solution)/shard_map/pallas_call | solution.py:71
  123.7 10.2 %shard_map.69.refs_2_ = f32[1024,1152]{1,0:T(8,128)} custom-call(f32[2]{0:T(128)S(1)} %pad_maximum_fusion.scalars, bf16[1024,1152]{1,0:T(8,128)(2,1)S(1)} %copy-done.1, s32[1024,1]{1,0:T(8,128)S(1)} %copy.9.row_ids, bf16[1024,1152]{1,0:T(8,128)(2,1)} %collective-permute-done.4.refs_0_, s32[1,1024]{1,0:T(1,128)S(1)} %get-tuple-element.6.refs_1_, ...), custom_call_target="tpu_custom_call" | custom-call | flops 4831838208 | bytes 9437184 | tf_op jit(solution)/shard_map/pallas_call | solution.py:71
  133.9 10.2 %shard_map.70 = f32[1024,1152]{1,0:T(8,128)} custom-call(f32[2]{0:T(128)S(1)} %pad_maximum_fusion.scalars, bf16[1024,1152]{1,0:T(8,128)(2,1)S(1)} %copy-done.1, s32[1024,1]{1,0:T(8,128)S(1)} %copy.9.row_ids, bf16[1024,1152]{1,0:T(8,128)(2,1)} %collective-permute-done.refs_0_, s32[1,1024]{1,0:T(1,128)S(1)} %bitcast.15, f32[1024,1152]{1,0:T(8,128)} %shard_map.69.refs_2_), custom_call_target="tpu_custom_call" | custom-call | flops 4831838208 | bytes 9437184 | tf_op jit(solution)/shard_map/pallas_call | solution.py:71
  144.2 0.0 collective-permute-done.7.refs_0_
  144.2 0.0 copy-start.3
  144.2 9.6 %shard_map.74 = bf16[1024,1152]{1,0:T(8,128)(2,1)S(1)} custom-call(f32[2]{0:T(128)S(1)} %pad_maximum_fusion.scalars, bf16[1024,1152]{1,0:T(8,128)(2,1)} %get-tuple-element.5.refs_0_.rows, s32[1024,1]{1,0:T(8,128)S(1)} %copy.13.row_ids, bf16[1024,1152]{1,0:T(8,128)(2,1)} %collective-permute-done.7.refs_0_, s32[1,1024]{1,0:T(1,128)S(1)} %get-tuple-element.7.refs_1_, ...), custom_call_target="tpu_custom_call" | custom-call | flops 4831838208 | bytes 9437184 | tf_op jit(solution)/shard_map/pallas_call | solution.py:71
  153.8 0.0 collective-permute-done.6
  153.8 0.0 copy-done.3
  153.8 3.3 %broadcast_select_fusion = (bf16[1024,1152]{1,0:T(8,128)(2,1)}, bf16[1024,1152]{1,0:T(8,128)(2,1)}) fusion(bf16[1024,1152]{1,0:T(8,128)(2,1)S(1)} %shard_map.74, pred[]{:T(512)S(6)} %eq.12, f32[1024,1152]{1,0:T(8,128)S(1)} %copy-done.3, bf16[1024,1152]{1,0:T(8,128)(2,1)S(1)} %collective-permute-done.6), kind=kLoop, calls=%fused_computation.1 | loop fusion | flops 5898240 | bytes 14155777 | tf_op jit(solution)/shard_map/jit(_where)/select_n | solution.py:137
  (4 shorter events, 0.0 us)
Async XLA Ops:
  0.6 57.8 %collective-permute-start.2 = (bf16[1024,1152]{1,0:T(8,128)(2,1)}, bf16[1024,1152]{1,0:T(8,128)(2,1)S(1)}, u32[]{:S(2)}, u32[]{:S(2)}) collective-permute-start(bf16[1024,1152]{1,0:T(8,128)(2,1)} %param.5), channel_id=1, source_target_pairs={{0,126},{2,0},{4,2},{6,4},{8,6},{10,8},{12,10},{14,12},{16,14},{18... | collective-permute-start | bytes 7077896 | tf_op jit(solution)/shard_map/ppermute | solution.py:94
  11.3 48.6 %collective-permute-start.3 = (bf16[1024,1152]{1,0:T(8,128)(2,1)}, bf16[1024,1152]{1,0:T(8,128)(2,1)}, u32[]{:S(2)}, u32[]{:S(2)}) collective-permute-start(bf16[1024,1152]{1,0:T(8,128)(2,1)} %param.6), channel_id=1, source_target_pairs={{1,3},{3,5},{5,7},{7,9},{9,11},{11,13},{13,15},{15,17},{17,19},{19... | collective-permute-start | bytes 7077896 | tf_op jit(solution)/shard_map/ppermute | solution.py:94
  18.4 44.0 %copy-start.5 = (s32[1024]{0:T(1024)S(1)}, s32[1024]{0:T(1024)}, u32[]{:S(2)}) copy-start(s32[1024]{0:T(1024)} %param.7) | copy-start | bytes 12292
  18.4 67.3 %collective-permute-start = (bf16[1024,1152]{1,0:T(8,128)(2,1)}, bf16[1024,1152]{1,0:T(8,128)(2,1)}, u32[]{:S(2)}, u32[]{:S(2)}) collective-permute-start(bf16[1024,1152]{1,0:T(8,128)(2,1)} %get-tuple-element.5.refs_0_.rows), channel_id=1, source_target_pairs={{0,2},{2,4},{4,6},{6,8},{8,10},{10,12},{12,14},{14,16},{16,18},{18... | collective-permute-start | bytes 7077896 | tf_op jit(solution)/shard_map/ppermute | solution.py:94
  58.5 1.4 copy-start.4
  61.8 24.3 %collective-permute-start.4 = (bf16[1024,1152]{1,0:T(8,128)(2,1)S(1)}, bf16[1024,1152]{1,0:T(8,128)(2,1)}, u32[]{:S(2)}, u32[]{:S(2)}) collective-permute-start(bf16[1024,1152]{1,0:T(8,128)(2,1)S(1)} %broadcast_select_fusion.2.rows.refs_0_), channel_id=1, source_target_pairs={{0,1},{1,0},{2,3},{3,2},{4,5},{5,4},{6,7},{7,6},{8,9},{9,8},{10,11... | collective-permute-start | bytes 7077896 | tf_op jit(solution)/shard_map/ppermute | solution.py:94
  61.9 35.1 %collective-permute-start.8 = (bf16[1024,1152]{1,0:T(8,128)(2,1)}, bf16[1024,1152]{1,0:T(8,128)(2,1)}, u32[]{:S(2)}, u32[]{:S(2)}) collective-permute-start(bf16[1024,1152]{1,0:T(8,128)(2,1)} %get-tuple-element.5.refs_0_.rows), channel_id=1, source_target_pairs={{0,1},{1,0},{2,3},{3,2},{4,5},{5,4},{6,7},{7,6},{8,9},{9,8},{10,11... | collective-permute-start | bytes 7077896 | tf_op jit(solution)/shard_map/ppermute | solution.py:94
  62.4 22.0 %collective-permute-start.1 = (s32[1024]{0:T(1024)S(1)}, s32[1024]{0:T(1024)S(1)}, u32[]{:S(2)}, u32[]{:S(2)}) collective-permute-start(s32[1024]{0:T(1024)S(1)} %copy-done.5), channel_id=1, source_target_pairs={{0,126},{1,127},{2,0},{3,1},{4,2},{5,3},{6,4},{7,5},{8,6},{9,7},{1... | collective-permute-start | bytes 12296 | tf_op jit(solution)/shard_map/ppermute | solution.py:94
  71.9 1.7 %copy-start = (bf16[1024,1152]{1,0:T(8,128)(2,1)S(1)}, bf16[1024,1152]{1,0:T(8,128)(2,1)}, u32[]{:S(2)}) copy-start(bf16[1024,1152]{1,0:T(8,128)(2,1)} %get-tuple-element.4.rows.refs_0_) | copy-start | bytes 7077892
  84.4 1.3 collective-permute-start.5
  85.7 58.5 %collective-permute-start.7 = (bf16[1024,1152]{1,0:T(8,128)(2,1)}, bf16[1024,1152]{1,0:T(8,128)(2,1)}, u32[]{:S(2)}, u32[]{:S(2)}) collective-permute-start(bf16[1024,1152]{1,0:T(8,128)(2,1)} %collective-permute-done.refs_0_), channel_id=1, source_target_pairs={{0,1},{1,0},{2,3},{3,2},{4,5},{5,4},{6,7},{7,6},{8,9},{9,8},{10,11... | collective-permute-start | bytes 7077896 | tf_op jit(solution)/shard_map/ppermute | solution.py:94
  86.1 1.0 copy-start.2
  87.2 9.9 %copy-start.1 = (bf16[1024,1152]{1,0:T(8,128)(2,1)S(1)}, bf16[1024,1152]{1,0:T(8,128)(2,1)}, u32[]{:S(2)}) copy-start(bf16[1024,1152]{1,0:T(8,128)(2,1)} %get-tuple-element.4.rows.refs_0_) | copy-start | bytes 7077892
  96.8 57.0 %collective-permute-start.6 = (bf16[1024,1152]{1,0:T(8,128)(2,1)S(1)}, bf16[1024,1152]{1,0:T(8,128)(2,1)S(1)}, u32[]{:S(2)}, u32[]{:S(2)}) collective-permute-start(bf16[1024,1152]{1,0:T(8,128)(2,1)S(1)} %shard_map.71), channel_id=1, source_target_pairs={{0,2},{2,4},{4,6},{6,8},{8,10},{10,12},{12,14},{14,16},{16,18},{18... | collective-permute-start | bytes 7077896 | tf_op jit(solution)/shard_map/ppermute | solution.py:94
  144.2 9.6 %copy-start.3 = (f32[1024,1152]{1,0:T(8,128)S(1)}, f32[1024,1152]{1,0:T(8,128)}, u32[]{:S(2)}) copy-start(f32[1024,1152]{1,0:T(8,128)} %shard_map.70) | copy-start | bytes 14155780

commit v2 on v1

v2 whole, which is shorter than its diff:
```python
import functools

import jax
import jax.numpy as jnp
from jax import lax
from jax.experimental import pallas as pl
from jax.experimental.pallas import tpu as pltpu
from jax.sharding import PartitionSpec as P

TILE = 512
PART = 256
LOG2_E = 1.4426950408889634


def band_kernel(pairs, has_sum, passes, scalars, rows, row_ids, *refs):
    cols = refs[: 2 * pairs]
    rest = refs[2 * pairs :]
    summed = rest[0] if has_sum else None
    out = rest[1] if has_sum else rest[0]
    scale = scalars[0]
    slope = -LOG2_E * scale
    start = -LOG2_E * scalars[1]
    work = [(r, p) for r in range(0, rows.shape[0], PART) for p in range(pairs)]

    def logits(item):
        r, p = item
        return lax.dot_general(
            rows[r : r + PART, :],
            cols[2 * p][...],
            (((1,), (1,)), ((), ())),
            preferred_element_type=jnp.float32,
        )

    ahead = logits(work[0])
    total = None
    for n, (r, p) in enumerate(work):
        now = ahead
        if n + 1 < len(work):
            ahead = logits(work[n + 1])
        hit = row_ids[r : r + PART, :] == cols[2 * p + 1][...]
        power = slope * now + start
        share = pl.reciprocal(1.0 + jnp.exp2(jnp.where(hit, -power, power)), approx=True)
        coef = (jnp.where(hit, -scale, scale) * share).astype(jnp.bfloat16)
        term = jnp.dot(coef, cols[2 * p][...], preferred_element_type=jnp.float32)
        if p == 0:
            total = summed[r : r + PART, :] + term if has_sum else term
        else:
            total = total + term
        if p == pairs - 1:
            out[r : r + PART, :] = total.astype(out.dtype)
    if passes:
        rest[-1][...] = rows[...]


def band(scalars, rows, row_ids, cols, summed=None, dtype=jnp.float32, passes=False):
    height, width = rows.shape
    pairs = len(cols)
    whole = lambda i: (0, 0)
    tile = lambda i: (i, 0)
    in_specs = [
        pl.BlockSpec(memory_space=pltpu.SMEM),
        pl.BlockSpec((TILE, width), tile),
        pl.BlockSpec((TILE, 1), tile),
    ]
    args = [scalars, rows, row_ids[:, None]]
    for col, col_ids in cols:
        in_specs += [pl.BlockSpec(col.shape, whole), pl.BlockSpec((1, col.shape[0]), whole)]
        args += [col, col_ids[None, :]]
    if summed is not None:
        in_specs.append(pl.BlockSpec((TILE, width), tile))
        args.append(summed)
    out_shape = [jax.ShapeDtypeStruct((height, width), dtype)]
    if passes:
        out_shape.append(jax.ShapeDtypeStruct((height, width), rows.dtype))
    flops = 4 * pairs * height * height * width
    results = pl.pallas_call(
        functools.partial(band_kernel, pairs, summed is not None, passes),
        grid=(height // TILE,),
        out_shape=out_shape,
        in_specs=in_specs,
        out_specs=[pl.BlockSpec((TILE, width), tile)] * len(out_shape),
        compiler_params=pltpu.CompilerParams(vmem_limit_bytes=40 * 1024 * 1024),
        cost_estimate=pl.CostEstimate(
            flops=flops, bytes_accessed=8 * height * width, transcendentals=pairs * height * height
        ),
    )(*args)
    return results if passes else results[0]


def shards(clips, captions, positive, log_scale, bias):
    rows = clips.shape[0]
    count = lax.axis_size("dp")
    mine = lax.axis_index("dp")
    even = mine % 2 == 0
    scalars = jnp.concatenate([jnp.exp(log_scale), bias])
    evens = range(0, count, 2)
    odds = range(1, count, 2)

    def move(value, pairs):
        return lax.ppermute(value, "dp", [(i, j % count) for i, j in pairs])

    def swap(value):
        return move(value, [(i, i ^ 1) for i in range(count)])

    apart = [(i, i - 2) for i in evens] + [(i, i + 2) for i in odds]
    home = [(i, i - 1) for i in evens] + [(i, i + 1) for i in odds]

    def caption_ids(owner):
        return (owner % count) * rows + jnp.arange(rows, dtype=jnp.int32)

    y = jnp.where(even, clips, captions)
    u1 = move(y, apart)
    y, clips, captions = lax.optimization_barrier((y, clips, captions))
    x = jnp.where(even, captions, clips)
    w = swap(x)
    u2 = move(w, apart)

    other_pos = swap(positive)
    chip_pos = jnp.stack([other_pos, positive])
    next_pos = jnp.where(
        even, move(chip_pos, [(i, i - 3) for i in odds]), move(chip_pos, [(i, i - 2) for i in odds])
    )
    x_ids = jnp.where(even, caption_ids(mine), positive)
    y_ids = jnp.where(even, positive, caption_ids(mine))
    w_ids = jnp.where(even, other_pos, caption_ids(mine - 1))
    u1_ids = jnp.where(even, next_pos[0], caption_ids(mine - 2))
    v1_ids = jnp.where(even, caption_ids(mine - 1), next_pos[0])
    u2_ids = jnp.where(even, next_pos[1], caption_ids(mine - 3))
    v2_ids = jnp.where(even, caption_ids(mine - 2), next_pos[1])

    gx = band(scalars, x, x_ids, [(y, y_ids)])
    gy = band(scalars, y, y_ids, [(x, x_ids)])
    gx = band(scalars, x, x_ids, [(w, w_ids)], gx)

    u1, gx, gy = lax.optimization_barrier((u1, gx, gy))
    v1 = swap(u1)
    gv = band(scalars, v1, v1_ids, [(u1, u1_ids)], dtype=jnp.bfloat16)
    back = move(gv, home)
    u1, v1, gv = lax.optimization_barrier((u1, v1, gv))
    gx = band(scalars, x, x_ids, [(u1, u1_ids)], gx)
    gy = band(scalars, y, y_ids, [(v1, v1_ids)], gy)

    u2, gx = lax.optimization_barrier((u2, gx))
    v2 = swap(u2)
    gx = band(scalars, x, x_ids, [(u2, u2_ids)], gx, dtype=jnp.bfloat16)
    gy = band(scalars, y, y_ids, [(v2, v2_ids)], gy)
    back, gx, gy = lax.optimization_barrier((back, gx, gy))
    gy = (gy + back.astype(jnp.float32)).astype(jnp.bfloat16)
    return jnp.where(even, gy, gx), jnp.where(even, gx, gy)


def solution(mesh):
    in_specs = (P("dp", None), P("dp", None), P("dp"), P(), P())
    out_specs = (P("dp", None), P("dp", None))
    return jax.shard_map(shards, mesh=mesh, in_specs=in_specs, out_specs=out_specs, check_vma=False)
```

time: 159 us -> 118 us (0.74)
  waiting for transfers between devices: 40.2 us -> 5.23 us
  Pallas kernels: 76.8 us -> 64.6 us
  local copies, waits for them, and re-layouts: 5.59 us -> 15.6 us
  other arithmetic: 10.3 us -> 7.16 us
    ppermute x9, waiting for transfers between devices: 40.2 us -> 5.23 us  [move(): return lax.ppermute(value, 'dp', [(i, j % count) for i, j in pairs])]
    pallas_call x7 -> x8, Pallas kernels: 76.8 us -> 64.6 us  [band(): pl.pallas_call(functools.partial(band_kernel, pairs, summed is not None,...]
    unnamed x12 -> x18, local copies, waits for them, and re-layouts: 4.14 us -> 14.1 us
    select_n x1, other arithmetic: 4.98 us -> 2.09 us  [shards(): y = jnp.where(even, clips, captions)]
  transfers between devices with their start and end apart: 9 -> 9, of which waited for: 2 -> 2; matrix products, arithmetic and copies ran while one was open for 5% -> 1% of each run, Pallas kernels for 49% -> 55%
where the time goes in v2:
time: 118 us
  Pallas kernels  64.6 us (55%)
  starting transfers between devices  22.8 us (19%)
  local copies, waits for them, and re-layouts  15.6 us (13%)
  other arithmetic  7.16 us (6%)
  waiting for transfers between devices  5.23 us (4%)
  between operations  2.24 us (2%)
    pallas_call x8, Pallas kernels, band(): pl.pallas_call(functools.partial(band_kernel, pairs, summed is not None,...  64.6 us
    ppermute x9, starting transfers between devices, move(): return lax.ppermute(value, 'dp', [(i, j % count) for i, j in pairs])  22.8 us
    unnamed x18, local copies, waits for them, and re-layouts  14.1 us
    ppermute x9, waiting for transfers between devices, move(): return lax.ppermute(value, 'dp', [(i, j % count) for i, j in pairs])  5.23 us
    select_n x1, other arithmetic, shards(): return (jnp.where(even, gy, gx), jnp.where(even, gx, gy))  3.23 us
  transfers between devices with their start and end apart: 9, of which 2 were waited for; matrix products, arithmetic and copies ran while one was open for 1% of the time, Pallas kernels for 55%

profile of v2, /device:TPU:0, one launch (start us, length us, event | category | flops | bytes accessed | tf_op | source)
XLA Modules:
  0.0 117.6 jit_solution(10573365745242833047)
XLA Ops:
  0.6 0.0 copy-start.6
  0.7 0.0 copy-start.7
  0.7 2.1 %broadcast_select_fusion.3.refs_0_.rows = bf16[1024,1152]{1,0:T(8,128)(2,1)S(1)} fusion(bf16[1024,1152]{1,0:T(8,128)(2,1)} %param.5, bf16[1024,1152]{1,0:T(8,128)(2,1)} %param.6, pred[]{:T(512)S(6)} %eq.12), kind=kLoop, calls=%fused_computation.4 | loop fusion | flops 1179648 | bytes 7077889 | tf_op jit(solution)/shard_map/jit(_where)/select_n | solution.py:111
  2.8 0.3 copy-done.6
  3.0 0.7 copy-done.7
  3.7 0.0 copy-start.8
  3.7 1.7 %broadcast_select_fusion.2.rows.refs_0_ = bf16[1024,1152]{1,0:T(8,128)(2,1)} fusion(bf16[1024,1152]{1,0:T(8,128)(2,1)S(1)} %copy-done.6, bf16[1024,1152]{1,0:T(8,128)(2,1)S(1)} %copy-done.7, pred[]{:T(512)S(6)} %eq.12), kind=kLoop, calls=%fused_computation.3 | loop fusion | flops 1179648 | bytes 7077889 | tf_op jit(solution)/shard_map/jit(_where)/select_n | solution.py:114
  5.4 0.0 collective-permute-start.1
  5.4 8.8 %collective-permute-start = (bf16[1024,1152]{1,0:T(8,128)(2,1)S(1)}, bf16[1024,1152]{1,0:T(8,128)(2,1)}, u32[]{:S(2)}, u32[]{:S(2)}) collective-permute-start(bf16[1024,1152]{1,0:T(8,128)(2,1)S(1)} %broadcast_select_fusion.3.refs_0_.rows), channel_id=1, source_target_pairs={{0,126},{2,0},{4,2},{6,4},{8,6},{10,8},{12,10},{14,12},{16,14},{18... | collective-permute-start | bytes 7077896 | tf_op jit(solution)/shard_map/ppermute | solution.py:100
  14.2 0.0 copy-done.8
  14.2 0.0 collective-permute-start.2
  15.5 0.2 copy.8.row_ids
  15.8 0.2 copy.9.row_ids
  16.0 0.1 pad_maximum_fusion.scalars
  16.1 7.6 %shard_map.70.refs_2_ = f32[1024,1152]{1,0:T(8,128)S(1)} custom-call(f32[2]{0:T(128)S(1)} %pad_maximum_fusion.scalars, bf16[1024,1152]{1,0:T(8,128)(2,1)S(1)} %broadcast_select_fusion.3.refs_0_.rows, s32[1024,1]{1,0:T(8,128)S(1)} %copy.9.row_ids, bf16[1024,1152]{1,0:T(8,128)(2,1)} %broadcast_select_fusion.2.rows.refs_0_, s32[1,1024]{1,0:T(1,128)S(1)} %bitcast.12), custom_call_target="tpu_custom_call" | custom-call | flops 4831838208 | bytes 9437184 | tf_op jit(solution)/shard_map/pallas_call | solution.py:76
  23.7 0.0 copy-start
  23.7 2.1 %copy-done = f32[1024,1152]{1,0:T(8,128)} copy-done((f32[1024,1152]{1,0:T(8,128)}, f32[1024,1152]{1,0:T(8,128)S(1)}, u32[]{:S(2)}) %copy-start) | copy-done | bytes 4718616
  25.8 7.2 %shard_map.68.refs_2_ = f32[1024,1152]{1,0:T(8,128)S(1)} custom-call(f32[2]{0:T(128)S(1)} %pad_maximum_fusion.scalars, bf16[1024,1152]{1,0:T(8,128)(2,1)} %broadcast_select_fusion.2.rows.refs_0_, s32[1024,1]{1,0:T(8,128)S(1)} %copy.8.row_ids, bf16[1024,1152]{1,0:T(8,128)(2,1)S(1)} %broadcast_select_fusion.3.refs_0_.rows, s32[1,1024]{1,0:T(1,128)S(1)} %bitcast.10), custom_call_target="tpu_custom_call" | custom-call | flops 4831838208 | bytes 9437184 | tf_op jit(solution)/shard_map/pallas_call | solution.py:76
  33.1 0.0 copy-start.2
  33.1 2.2 %copy-done.2 = f32[1024,1152]{1,0:T(8,128)} copy-done((f32[1024,1152]{1,0:T(8,128)}, f32[1024,1152]{1,0:T(8,128)S(1)}, u32[]{:S(2)}) %copy-start.2) | copy-done | bytes 4718616
  35.2 0.0 collective-permute-done.2
  35.3 0.0 collective-permute-done.1.refs_0_
  35.3 8.8 %shard_map.69.refs_2_ = f32[1024,1152]{1,0:T(8,128)S(1)} custom-call(f32[2]{0:T(128)S(1)} %pad_maximum_fusion.scalars, bf16[1024,1152]{1,0:T(8,128)(2,1)} %broadcast_select_fusion.2.rows.refs_0_, s32[1024,1]{1,0:T(8,128)S(1)} %copy.8.row_ids, bf16[1024,1152]{1,0:T(8,128)(2,1)} %collective-permute-done.1.refs_0_, s32[1,1024]{1,0:T(1,128)S(1)} %bitcast.13, ...), custom_call_target="tpu_custom_call" | custom-call | flops 4831838208 | bytes 9437184 | tf_op jit(solution)/shard_map/pallas_call | solution.py:76
  44.0 0.0 copy-start.1
  44.0 2.2 %copy-done.1 = f32[1024,1152]{1,0:T(8,128)} copy-done((f32[1024,1152]{1,0:T(8,128)}, f32[1024,1152]{1,0:T(8,128)S(1)}, u32[]{:S(2)}) %copy-start.1) | copy-done | bytes 4718616
  46.2 0.0 collective-permute-done.refs_0_
  46.2 0.5 collective-permute-start.3
  46.7 1.8 %collective-permute-start.7 = (bf16[1024,1152]{1,0:T(8,128)(2,1)}, bf16[1024,1152]{1,0:T(8,128)(2,1)}, u32[]{:S(2)}, u32[]{:S(2)}) collective-permute-start(bf16[1024,1152]{1,0:T(8,128)(2,1)} %collective-permute-done.1.refs_0_), channel_id=1, source_target_pairs={{0,126},{2,0},{4,2},{6,4},{8,6},{10,8},{12,10},{14,12},{16,14},{18... | collective-permute-start | bytes 7077896 | tf_op jit(solution)/shard_map/ppermute | solution.py:100
  48.6 0.7 collective-permute-start.5
  49.2 1.5 %collective-permute-start.4 = (s32[2,1024]{1,0:T(2,128)S(1)}, s32[2,1024]{1,0:T(2,128)S(1)}, u32[]{:S(2)}, u32[]{:S(2)}) collective-permute-start(s32[2,1024]{1,0:T(2,128)S(1)} %pad_add_fusion), channel_id=1, source_target_pairs={{1,126},{3,0},{5,2},{7,4},{9,6},{11,8},{13,10},{15,12},{17,14},{19... | collective-permute-start | bytes 24584 | tf_op jit(solution)/shard_map/ppermute | solution.py:100
  50.7 0.0 collective-permute-done.5
  50.8 3.6 %collective-permute-done.4 = s32[2,1024]{1,0:T(2,128)S(1)} collective-permute-done((s32[2,1024]{1,0:T(2,128)S(1)}, s32[2,1024]{1,0:T(2,128)S(1)}, u32[]{:S(2)}, u32[]{:S(2)}) %collective-permute-start.4) | collective-permute-done | bytes 8224 | tf_op jit(solution)/shard_map/ppermute | solution.py:100
  54.4 1.0 copy.10
  55.4 0.1 add_select_fusion.row_ids
  55.5 0.0 collective-permute-done.3.rows.refs_0_
  55.5 8.0 %shard_map.71 = bf16[1024,1152]{1,0:T(8,128)(2,1)S(1)} custom-call(f32[2]{0:T(128)S(1)} %pad_maximum_fusion.scalars, bf16[1024,1152]{1,0:T(8,128)(2,1)} %collective-permute-done.3.rows.refs_0_, s32[1024,1]{1,0:T(8,128)S(1)} %add_select_fusion.row_ids, bf16[1024,1152]{1,0:T(8,128)(2,1)} %collective-permute-done.refs_0_, s32[1,1024]{1,0:T(1,128)S(1)} %get-tuple-element.34.refs_1_), custom_call_target="tpu_custom_call" | custom-call | flops 4831838208 | bytes 9437184 | tf_op jit(solution)/shard_map/pallas_call | solution.py:76
  63.5 8.8 %shard_map.72.refs_2_ = f32[1024,1152]{1,0:T(8,128)S(1)} custom-call(f32[2]{0:T(128)S(1)} %pad_maximum_fusion.scalars, bf16[1024,1152]{1,0:T(8,128)(2,1)} %broadcast_select_fusion.2.rows.refs_0_, s32[1024,1]{1,0:T(8,128)S(1)} %copy.8.row_ids, bf16[1024,1152]{1,0:T(8,128)(2,1)} %collective-permute-done.refs_0_, s32[1,1024]{1,0:T(1,128)S(1)} %get-tuple-element.34.refs_1_, ...), custom_call_target="tpu_custom_call" | custom-call | flops 4831838208 | bytes 9437184 | tf_op jit(solution)/shard_map/pallas_call | solution.py:76
  72.2 0.0 copy-start.3
  72.3 2.2 %copy-done.3 = f32[1024,1152]{1,0:T(8,128)} copy-done((f32[1024,1152]{1,0:T(8,128)}, f32[1024,1152]{1,0:T(8,128)S(1)}, u32[]{:S(2)}) %copy-start.3) | copy-done | bytes 4718616
  74.4 1.6 %collective-permute-done.7.refs_0_ = bf16[1024,1152]{1,0:T(8,128)(2,1)} collective-permute-done((bf16[1024,1152]{1,0:T(8,128)(2,1)}, bf16[1024,1152]{1,0:T(8,128)(2,1)}, u32[]{:S(2)}, u32[]{:S(2)}) %collective-permute-start.7) | collective-permute-done | bytes 2359328 | tf_op jit(solution)/shard_map/ppermute | solution.py:100
  76.1 4.1 %collective-permute-start.8 = (bf16[1024,1152]{1,0:T(8,128)(2,1)}, bf16[1024,1152]{1,0:T(8,128)(2,1)S(1)}, u32[]{:S(2)}, u32[]{:S(2)}) collective-permute-start(bf16[1024,1152]{1,0:T(8,128)(2,1)} %collective-permute-done.7.refs_0_), channel_id=1, source_target_pairs={{0,1},{1,0},{2,3},{3,2},{4,5},{5,4},{6,7},{7,6},{8,9},{9,8},{10,11... | collective-permute-start | bytes 7077896 | tf_op jit(solution)/shard_map/ppermute | solution.py:100
  80.2 5.4 %collective-permute-start.6 = (bf16[1024,1152]{1,0:T(8,128)(2,1)S(1)}, bf16[1024,1152]{1,0:T(8,128)(2,1)S(1)}, u32[]{:S(2)}, u32[]{:S(2)}) collective-permute-start(bf16[1024,1152]{1,0:T(8,128)(2,1)S(1)} %shard_map.71), channel_id=1, source_target_pairs={{0,127},{2,1},{4,3},{6,5},{8,7},{10,9},{12,11},{14,13},{16,15},{18... | collective-permute-start | bytes 7077896 | tf_op jit(solution)/shard_map/ppermute | solution.py:100
  85.6 0.0 copy-start.4
  85.6 2.3 %copy-done.4 = f32[1024,1152]{1,0:T(8,128)S(1)} copy-done((f32[1024,1152]{1,0:T(8,128)S(1)}, f32[1024,1152]{1,0:T(8,128)}, u32[]{:S(2)}) %copy-start.4) | copy-done | bytes 4718616
  87.9 8.1 %shard_map.73 = bf16[1024,1152]{1,0:T(8,128)(2,1)S(1)} custom-call(f32[2]{0:T(128)S(1)} %pad_maximum_fusion.scalars, bf16[1024,1152]{1,0:T(8,128)(2,1)} %broadcast_select_fusion.2.rows.refs_0_, s32[1024,1]{1,0:T(8,128)S(1)} %copy.8.row_ids, bf16[1024,1152]{1,0:T(8,128)(2,1)} %collective-permute-done.7.refs_0_, s32[1,1024]{1,0:T(1,128)S(1)} %get-tuple-element.32.refs_1_, ...), custom_call_target="tpu_custom_call" | custom-call | flops 4831838208 | bytes 9437184 | tf_op jit(solution)/shard_map/pallas_call | solution.py:76
  96.0 8.4 %shard_map.74.refs_2_ = f32[1024,1152]{1,0:T(8,128)S(1)} custom-call(f32[2]{0:T(128)S(1)} %pad_maximum_fusion.scalars, bf16[1024,1152]{1,0:T(8,128)(2,1)S(1)} %broadcast_select_fusion.3.refs_0_.rows, s32[1024,1]{1,0:T(8,128)S(1)} %copy.9.row_ids, bf16[1024,1152]{1,0:T(8,128)(2,1)} %collective-permute-done.3.rows.refs_0_, ...), custom_call_target="tpu_custom_call" | custom-call | flops 4831838208 | bytes 9437184 | tf_op jit(solution)/shard_map/pallas_call | solution.py:76
  104.4 0.0 copy-start.5
  104.4 2.1 %copy-done.5 = f32[1024,1152]{1,0:T(8,128)} copy-done((f32[1024,1152]{1,0:T(8,128)}, f32[1024,1152]{1,0:T(8,128)S(1)}, u32[]{:S(2)}) %copy-start.5) | copy-done | bytes 4718616
  106.5 0.0 collective-permute-done.8.refs_0_
  106.5 7.8 %shard_map.75 = f32[1024,1152]{1,0:T(8,128)S(1)} custom-call(f32[2]{0:T(128)S(1)} %pad_maximum_fusion.scalars, bf16[1024,1152]{1,0:T(8,128)(2,1)S(1)} %broadcast_select_fusion.3.refs_0_.rows, s32[1024,1]{1,0:T(8,128)S(1)} %copy.9.row_ids, bf16[1024,1152]{1,0:T(8,128)(2,1)S(1)} %collective-permute-done.8.refs_0_, s32[1,1024]{1,0:T(1,128)S(1)} %get-tuple-element.33.refs_1_, ...), custom_call_target="tpu_custom_call" | custom-call | flops 4831838208 | bytes 9437184 | tf_op jit(solution)/shard_map/pallas_call | solution.py:76
  114.3 0.0 collective-permute-done.6
  114.3 3.2 %broadcast_select_fusion = (bf16[1024,1152]{1,0:T(8,128)(2,1)}, bf16[1024,1152]{1,0:T(8,128)(2,1)}) fusion(bf16[1024,1152]{1,0:T(8,128)(2,1)S(1)} %shard_map.73, pred[]{:T(512)S(6)} %eq.12, f32[1024,1152]{1,0:T(8,128)S(1)} %shard_map.75, bf16[1024,1152]{1,0:T(8,128)(2,1)S(1)} %collective-permute-done.6), kind=kLoop, calls=%fused_computation.1 | loop fusion | flops 5898240 | bytes 14155777 | tf_op jit(solution)/shard_map/jit(_where)/select_n | solution.py:149
  (5 shorter events, 0.0 us)
Async XLA Ops:
  0.6 2.4 %copy-start.6 = (bf16[1024,1152]{1,0:T(8,128)(2,1)S(1)}, bf16[1024,1152]{1,0:T(8,128)(2,1)}, u32[]{:S(2)}) copy-start(bf16[1024,1152]{1,0:T(8,128)(2,1)} %param.6) | copy-start | bytes 7077892
  0.7 3.1 %copy-start.7 = (bf16[1024,1152]{1,0:T(8,128)(2,1)S(1)}, bf16[1024,1152]{1,0:T(8,128)(2,1)}, u32[]{:S(2)}) copy-start(bf16[1024,1152]{1,0:T(8,128)(2,1)} %param.5) | copy-start | bytes 7077892
  3.7 10.4 %copy-start.8 = (s32[1024]{0:T(1024)S(1)}, s32[1024]{0:T(1024)}, u32[]{:S(2)}) copy-start(s32[1024]{0:T(1024)} %param.7) | copy-start | bytes 12292
  5.4 29.9 %collective-permute-start.1 = (bf16[1024,1152]{1,0:T(8,128)(2,1)}, bf16[1024,1152]{1,0:T(8,128)(2,1)}, u32[]{:S(2)}, u32[]{:S(2)}) collective-permute-start(bf16[1024,1152]{1,0:T(8,128)(2,1)} %broadcast_select_fusion.2.rows.refs_0_), channel_id=1, source_target_pairs={{0,1},{1,0},{2,3},{3,2},{4,5},{5,4},{6,7},{7,6},{8,9},{9,8},{10,11... | collective-permute-start | bytes 7077896 | tf_op jit(solution)/shard_map/ppermute | solution.py:100
  5.4 40.8 %collective-permute-start = (bf16[1024,1152]{1,0:T(8,128)(2,1)S(1)}, bf16[1024,1152]{1,0:T(8,128)(2,1)}, u32[]{:S(2)}, u32[]{:S(2)}) collective-permute-start(bf16[1024,1152]{1,0:T(8,128)(2,1)S(1)} %broadcast_select_fusion.3.refs_0_.rows), channel_id=1, source_target_pairs={{0,126},{2,0},{4,2},{6,4},{8,6},{10,8},{12,10},{14,12},{16,14},{18... | collective-permute-start | bytes 7077896 | tf_op jit(solution)/shard_map/ppermute | solution.py:100
  14.2 21.1 %collective-permute-start.2 = (s32[1024]{0:T(1024)S(1)}, s32[1024]{0:T(1024)S(1)}, u32[]{:S(2)}, u32[]{:S(2)}) collective-permute-start(s32[1024]{0:T(1024)S(1)} %copy-done.8), channel_id=1, source_target_pairs={{0,1},{1,0},{2,3},{3,2},{4,5},{5,4},{6,7},{7,6},{8,9},{9,8},{10,11... | collective-permute-start | bytes 12296 | tf_op jit(solution)/shard_map/ppermute | solution.py:100
  23.7 2.1 %copy-start = (f32[1024,1152]{1,0:T(8,128)}, f32[1024,1152]{1,0:T(8,128)S(1)}, u32[]{:S(2)}) copy-start(f32[1024,1152]{1,0:T(8,128)S(1)} %shard_map.70.refs_2_) | copy-start | bytes 14155780
  33.1 2.2 %copy-start.2 = (f32[1024,1152]{1,0:T(8,128)}, f32[1024,1152]{1,0:T(8,128)S(1)}, u32[]{:S(2)}) copy-start(f32[1024,1152]{1,0:T(8,128)S(1)} %shard_map.68.refs_2_) | copy-start | bytes 14155780
  44.0 2.2 %copy-start.1 = (f32[1024,1152]{1,0:T(8,128)}, f32[1024,1152]{1,0:T(8,128)S(1)}, u32[]{:S(2)}) copy-start(f32[1024,1152]{1,0:T(8,128)S(1)} %shard_map.69.refs_2_) | copy-start | bytes 14155780
  46.2 9.3 %collective-permute-start.3 = (bf16[1024,1152]{1,0:T(8,128)(2,1)}, bf16[1024,1152]{1,0:T(8,128)(2,1)}, u32[]{:S(2)}, u32[]{:S(2)}) collective-permute-start(bf16[1024,1152]{1,0:T(8,128)(2,1)} %collective-permute-done.refs_0_), channel_id=1, source_target_pairs={{0,1},{1,0},{2,3},{3,2},{4,5},{5,4},{6,7},{7,6},{8,9},{9,8},{10,11... | collective-permute-start | bytes 7077896 | tf_op jit(solution)/shard_map/ppermute | solution.py:100
  46.7 29.3 %collective-permute-start.7 = (bf16[1024,1152]{1,0:T(8,128)(2,1)}, bf16[1024,1152]{1,0:T(8,128)(2,1)}, u32[]{:S(2)}, u32[]{:S(2)}) collective-permute-start(bf16[1024,1152]{1,0:T(8,128)(2,1)} %collective-permute-done.1.refs_0_), channel_id=1, source_target_pairs={{0,126},{2,0},{4,2},{6,4},{8,6},{10,8},{12,10},{14,12},{16,14},{18... | collective-permute-start | bytes 7077896 | tf_op jit(solution)/shard_map/ppermute | solution.py:100
  48.6 2.2 %collective-permute-start.5 = (s32[2,1024]{1,0:T(2,128)S(1)}, s32[2,1024]{1,0:T(2,128)S(1)}, u32[]{:S(2)}, u32[]{:S(2)}) collective-permute-start(s32[2,1024]{1,0:T(2,128)S(1)} %pad_add_fusion), channel_id=1, source_target_pairs={{1,127},{3,1},{5,3},{7,5},{9,7},{11,9},{13,11},{15,13},{17,15},{19... | collective-permute-start | bytes 24584 | tf_op jit(solution)/shard_map/ppermute | solution.py:100
  49.2 5.1 %collective-permute-start.4 = (s32[2,1024]{1,0:T(2,128)S(1)}, s32[2,1024]{1,0:T(2,128)S(1)}, u32[]{:S(2)}, u32[]{:S(2)}) collective-permute-start(s32[2,1024]{1,0:T(2,128)S(1)} %pad_add_fusion), channel_id=1, source_target_pairs={{1,126},{3,0},{5,2},{7,4},{9,6},{11,8},{13,10},{15,12},{17,14},{19... | collective-permute-start | bytes 24584 | tf_op jit(solution)/shard_map/ppermute | solution.py:100
  72.2 2.2 %copy-start.3 = (f32[1024,1152]{1,0:T(8,128)}, f32[1024,1152]{1,0:T(8,128)S(1)}, u32[]{:S(2)}) copy-start(f32[1024,1152]{1,0:T(8,128)S(1)} %shard_map.72.refs_2_) | copy-start | bytes 14155780
  76.1 30.4 %collective-permute-start.8 = (bf16[1024,1152]{1,0:T(8,128)(2,1)}, bf16[1024,1152]{1,0:T(8,128)(2,1)S(1)}, u32[]{:S(2)}, u32[]{:S(2)}) collective-permute-start(bf16[1024,1152]{1,0:T(8,128)(2,1)} %collective-permute-done.7.refs_0_), channel_id=1, source_target_pairs={{0,1},{1,0},{2,3},{3,2},{4,5},{5,4},{6,7},{7,6},{8,9},{9,8},{10,11... | collective-permute-start | bytes 7077896 | tf_op jit(solution)/shard_map/ppermute | solution.py:100
  80.2 34.2 %collective-permute-start.6 = (bf16[1024,1152]{1,0:T(8,128)(2,1)S(1)}, bf16[1024,1152]{1,0:T(8,128)(2,1)S(1)}, u32[]{:S(2)}, u32[]{:S(2)}) collective-permute-start(bf16[1024,1152]{1,0:T(8,128)(2,1)S(1)} %shard_map.71), channel_id=1, source_target_pairs={{0,127},{2,1},{4,3},{6,5},{8,7},{10,9},{12,11},{14,13},{16,15},{18... | collective-permute-start | bytes 7077896 | tf_op jit(solution)/shard_map/ppermute | solution.py:100
  85.6 2.3 %copy-start.4 = (f32[1024,1152]{1,0:T(8,128)S(1)}, f32[1024,1152]{1,0:T(8,128)}, u32[]{:S(2)}) copy-start(f32[1024,1152]{1,0:T(8,128)} %copy-done.3) | copy-start | bytes 14155780
  104.4 2.1 %copy-start.5 = (f32[1024,1152]{1,0:T(8,128)}, f32[1024,1152]{1,0:T(8,128)S(1)}, u32[]{:S(2)}) copy-start(f32[1024,1152]{1,0:T(8,128)S(1)} %shard_map.74.refs_2_) | copy-start | bytes 14155780
